TPU v7x, 256 devices: a whole 4x4x8 slice. The times are simulated.
256 devices in a mesh: dp: 16 (over x_lo, y, core), shard: 16 (over x_hi, z).
Axes of the slice: x: 4 (x_hi: 2, x_lo: 2; x = x_hi * 2 + x_lo), y: 4, z: 8, core: 2. Of those that a mesh axis runs over, the one named last changes fastest.
Arguments:
- inputs: bfloat16 [32768, 8192], P(('dp', 'shard')), may hold values from -6 to 6
- cotangent: bfloat16 [32768, 1024], P(('dp', 'shard')), may hold values from -160 to 160
- weight: bfloat16 [8192, 1024], P('shard'), may hold values from -0.0625 to 0.0625
- projector: bfloat16 [8192, 1024], P('shard'), may hold values from -0.0625 to 0.0625
- first_moment_state: float32 [1024, 1024], P(('dp', 'shard')), may hold values from -6 to 6
- second_moment_state: float32 [1024, 1024], P(('dp', 'shard')), may hold values from 0.25 to 4
Outputs:
- input_gradient: bfloat16 [32768, 8192], P(('dp', 'shard'))
- weight_update: bfloat16 [8192, 1024], P('shard')
- new_first: float32 [1024, 1024], P(('dp', 'shard'))
- new_second: float32 [1024, 1024], P(('dp', 'shard'))
All inputs are finite; a program needn't handle non-finite values.
Results may differ from a plain program's by a relative error of at most 0.009.
Values may be sent and summed in bfloat16 or wider, within the bound.
A program may use at most 128 MiB of HBM per device.

v0:
```python
import jax
import jax.numpy as jnp
from jax import lax
from jax.sharding import PartitionSpec as P

KEY_OUTPUTS = 1024
PROJECTION_RANK = 1024


beta_one = 0.9
beta_two = 0.999
bias_one = 1.0
bias_two = 0.632304575


def local(inputs, cotangent, weight, projector, first_moment_state, second_moment_state):
    split_inputs = lax.all_to_all(inputs, "shard", split_axis=1, concat_axis=0, tiled=True)
    part_term = jnp.dot(split_inputs, projector, preferred_element_type=jnp.float32)
    projected = lax.psum_scatter(
        lax.optimization_barrier(part_term.astype(jnp.bfloat16))
        .astype(jnp.float32)
        .astype(jnp.bfloat16),
        "shard",
        scatter_dimension=0,
        tiled=True,
    ).astype(jnp.float32)
    columns = cotangent.astype(jnp.float32)
    key_gradient = lax.psum_scatter(
        lax.dot_general(
            columns,
            projected,
            (((0,), (0,)), ((), ())),
            precision=lax.Precision.HIGHEST,
            preferred_element_type=jnp.float32,
        ),
        ("dp", "shard"),
        scatter_dimension=0,
        tiled=True,
    )
    squared_total = lax.psum(jnp.sum(key_gradient * key_gradient), ("dp", "shard"))
    step_factor = jnp.minimum(
        1.0, lax.rsqrt(squared_total / (KEY_OUTPUTS * PROJECTION_RANK) + 1e-06)
    )
    clipped = key_gradient * step_factor
    new_first = beta_one * first_moment_state + (1.0 - beta_one) * clipped
    new_second = beta_two * second_moment_state + (1.0 - beta_two) * clipped * clipped
    direction = (new_first / bias_one / (jnp.sqrt(new_second / bias_two) + 1e-08)).astype(
        jnp.bfloat16
    )
    weight_update = lax.dot_general(
        projector,
        lax.all_gather(direction, ("dp", "shard"), axis=0, tiled=True),
        (((1,), (1,)), ((), ())),
        preferred_element_type=jnp.float32,
    ).astype(jnp.bfloat16)
    input_gradient = lax.dot_general(
        cotangent,
        lax.all_gather(weight, "shard", axis=0, tiled=True),
        (((1,), (1,)), ((), ())),
        preferred_element_type=jnp.float32,
    ).astype(jnp.bfloat16)
    return (input_gradient, weight_update, new_first, new_second)


def solution(mesh):
    return jax.shard_map(
        local,
        mesh=mesh,
        in_specs=(
            P(("dp", "shard"), None),
            P(("dp", "shard"), None),
            P("shard", None),
            P("shard", None),
            P(("dp", "shard"), None),
            P(("dp", "shard"), None),
        ),
        out_specs=(
            P(("dp", "shard"), None),
            P("shard", None),
            P(("dp", "shard"), None),
            P(("dp", "shard"), None),
        ),
        check_vma=False,
    )
```

profile of v0, /device:TPU:1, one launch (start us, length us, event | category | flops | bytes accessed | tf_op | source)
XLA Modules:
  0.0 1576.8 jit_solution(10767097952122253240)
XLA Ops:
  7.2 0.0 reduce-scatter.3.cloned.1.call-start
  7.2 4.1 copy.45
  11.4 60.5 %all_to_all.19 = bf16[128,16,512]{0,2,1:T(8,128)(2,1)S(1)} all-to-all(bf16[128,16,512]{0,2,1:T(8,128)(2,1)} %bitcast.20), channel_id=1, replica_groups=mesh['dp'=16,'shard'=16] {'shard'}, dimensions={1} | all-to-all | bytes 4194304 | tf_op jit(solution)/shard_map/all_to_all | solution.py:17
  71.9 2.6 copy.46
  74.5 5.9 convolution_convert_fusion.1
  80.4 0.0 reduce-scatter.3.cloned.1.call-update
  80.4 0.0 all-reduce.3.cloned.1.call-start
  80.4 202.8 %reduce-scatter.3.cloned.1.call-done = bf16[128,1024]{1,0:T(8,128)(2,1)} async-done(((bf16[2048,1024]{1,0:T(8,128)(2,1)}), bf16[128,1024]{1,0:T(8,128)(2,1)}) %reduce-scatter.3.cloned.1.call-update) | async-done | bytes 262160 | tf_op jit(solution)/shard_map/reduce_scatter | solution.py:19
  283.2 3.6 convolution_bitcast_fusion
  286.8 0.0 all-reduce.3.cloned.1.call-update
  286.9 0.0 all-gather.6.cloned.1.call-start
  286.9 272.3 %all-reduce.3.cloned.1.call-done = f32[1024,1024]{0,1:T(8,128)} async-done(((f32[1024,1024]{0,1:T(8,128)}), f32[1024,1024]{0,1:T(8,128)}) %all-reduce.3.cloned.1.call-update) | async-done | bytes 4194320
  559.2 1.9 multiply_reduce_fusion
  561.1 0.2 copy.47
  561.2 77.7 %psum.7 = f32[]{:T(128)} all-reduce(f32[]{:T(128)} %get-tuple-element.27), channel_id=1, replica_groups=mesh['dp'=16,'shard'=16] {'dp','shard'}, use_global_device_ids=true, to_apply=%region_3.0 | all-reduce | flops 1 | bytes 8 | tf_op jit(solution)/shard_map/psum | solution.py:40
  639.7 0.6 fusion.3
  640.3 0.0 all-gather.4.cloned.1.call-start
  640.4 0.5 all-gather.4.cloned.1.call-update
  640.9 690.5 %all-gather.6.cloned.1.call-done = bf16[256,4,1024]{2,1,0:T(4,128)(2,1)} async-done(((bf16[1,4,1024]{2,1,0:T(4,128)(2,1)}), bf16[256,4,1024]{2,1,0:T(4,128)(2,1)}) %all-gather.6.cloned.1.call-update) | async-done | bytes 2097168 | tf_op jit(solution)/shard_map/all_gather | solution.py:52
  1331.4 2.5 reshape.12
  1334.0 2.3 fusion
  1336.2 2.3 copy.48
  1338.5 219.1 %all-gather.4.cloned.1.call-done = bf16[8192,1024]{1,0:T(8,128)(2,1)} async-done(((bf16[512,1024]{1,0:T(8,128)(2,1)}), bf16[8192,1024]{1,0:T(8,128)(2,1)}) %all-gather.4.cloned.1.call-update) | async-done | bytes 16777232 | tf_op jit(solution)/shard_map/all_gather | solution.py:58
  1557.6 12.7 convolution_convert_fusion
  (9 shorter events, 0.0 us)
Async XLA Ops:
  7.2 67.3 %copy-start = (bf16[512,1024]{1,0:T(8,128)(2,1)S(1)}, bf16[512,1024]{1,0:T(8,128)(2,1)}, u32[]{:S(2)}) copy-start(bf16[512,1024]{1,0:T(8,128)(2,1)} %param.9) | copy-start | bytes 3145732
  7.2 276.0 %reduce-scatter.3.cloned.1.call-start = ((), (), s32[]{:S(2)}) async-start(), calls=%async_computation.3 | async-start | bytes 4456448 | tf_op jit(solution)/shard_map/reduce_scatter | solution.py:19
  80.4 202.9 %copy-start.1 = (bf16[128,1024]{1,0:T(8,128)(2,1)S(1)}, bf16[128,1024]{1,0:T(8,128)(2,1)}, u32[]{:S(2)}) copy-start(bf16[128,1024]{1,0:T(8,128)(2,1)} %param.7) | copy-start | bytes 786436
  80.4 478.8 %all-reduce.3.cloned.1.call-start = ((), (), s32[]{:S(2)}) async-start(), calls=%async_computation.5 | async-start | bytes 8388608
  286.8 352.8 %copy-start.2 = (f32[4,1024]{1,0:T(4,128)S(1)}, f32[4,1024]{1,0:T(4,128)}, u32[]{:S(2)}) copy-start(f32[4,1024]{1,0:T(4,128)} %param.11) | copy-start | bytes 49156
  286.8 352.8 %copy-start.3 = (f32[4,1024]{1,0:T(4,128)S(1)}, f32[4,1024]{1,0:T(4,128)}, u32[]{:S(2)}) copy-start(f32[4,1024]{1,0:T(4,128)} %param.10) | copy-start | bytes 49156
  286.9 1044.6 %all-gather.6.cloned.1.call-start = ((), (), s32[]{:S(2)}) async-start(), calls=%async_computation.4 | async-start | bytes 2105344 | tf_op jit(solution)/shard_map/all_gather | solution.py:52
  640.3 917.2 %all-gather.4.cloned.1.call-start = ((), (), s32[]{:S(2)}) async-start(), calls=%async_computation.2 | async-start | bytes 17825792 | tf_op jit(solution)/shard_map/all_gather | solution.py:58
Sparse Core Ops, SparseCore 0:
  80.5 202.6 reduce-scatter.2
  289.6 269.5 all-reduce.2
  640.4 690.9 all-gather.5
  1333.9 223.6 all-gather.3
where the time goes:
time: 1580 us
  waiting for transfers between devices  1390 us (88%)
  blocking collectives  138 us (9%)
  matrix products  24.5 us (2%)
    all_gather x1, waiting for transfers between devices, local(): lax.all_gather(direction, ('dp', 'shard'), axis=0, tiled=True)  691 us
    unnamed x5, waiting for transfers between devices  273 us
    all_gather x1, waiting for transfers between devices, local(): lax.all_gather(weight, 'shard', axis=0, tiled=True)  219 us
    reduce_scatter x1, waiting for transfers between devices, local(): lax.psum_scatter(lax.optimization_barrier(part_term.astype(jnp.bfloat16))...  203 us
    psum x1, blocking collectives, local(): lax.psum(jnp.sum(key_gradient * key_gradient), ('dp', 'shard'))  77.7 us
    all_to_all x1, blocking collectives, local(): lax.all_to_all(inputs, 'shard', split_axis=1, concat_axis=0, tiled=True)  60.5 us
  transfers between devices with their start and end apart: 4, of which 4 were waited for; matrix products, arithmetic and copies ran while one was open for 0% of the time, Pallas kernels for 0%

commit v1 on v0

v1 whole, which is shorter than its diff:
```python
import jax
import jax.numpy as jnp
from jax import lax
from jax.experimental import pallas as pl
from jax.experimental.pallas import tpu as pltpu
from jax.sharding import PartitionSpec as P

MESH = pl.DeviceIdType.MESH
F32 = jnp.float32
BF16 = jnp.bfloat16

TOKENS = 128
WIDTH = 8192
OUTS = 1024
RANK = 1024
ENTRIES = OUTS * RANK

beta_one = 0.9
beta_two = 0.999
bias_one = 1.0
bias_two = 0.632304575

NN = (((1,), (0,)), ((), ()))
NT = (((1,), (1,)), ((), ()))


def dot(a, b, dims=NN):
    return lax.dot_general(a, b, dims, preferred_element_type=F32)


def flip(bit, by):
    return 1 - bit if by else bit


def wait_bytes(ref, sem):
    pltpu.make_async_copy(ref, ref, sem).wait()


PAIRS = ((0, 0), (0, 1), (1, 0), (1, 1))
ORDER = (1, 3, 2)


def kernel(
    inp, cot, w, p, m_in, v_in,
    ig, wu, nf, nv,
    cx, cy, ct, xx, pg, wg, pblk, mf, mb, igb,
    s0, r0, a_keep, a0, a1, ra0, ra1, b0, b1, rb0, rb1, cs, rc, gz, mvz, ss, sr_a, sr_b, df, dall,
    local_sem, c_send, c_recv, x_send, x_recv, pre_send, pre_recv,
    ring_send_sem, ring_recv_sem, mv_send, mv_recv, o_send, o_recv,
    s_send, s_recv, a_send, a_recv, b_send, b_recv, z_send, z_recv, g_send, g_recv,
    q_send, q_recv, d_send, d_recv, e_send, e_recv,
):
    d = lax.axis_index("dp")
    s = lax.axis_index("shard")
    xl = d // 8
    y = (d // 2) % 4
    yh = y // 2
    yl = y % 2
    c = d % 2
    h = s // 8
    z = s % 8

    def device(xl_, yh_, yl_, c_, h_, z_):
        return ((xl_ * 4 + yh_ * 2 + yl_) * 2 + c_, h_ * 8 + z_)

    def partner(axis, i, kc):
        hi, lo = PAIRS[i]
        if axis == 0:
            return device(flip(xl, lo), yh, yl, flip(c, kc), flip(h, hi), z)
        return device(xl, flip(yh, hi), flip(yl, lo), flip(c, kc), h, z)

    def z_peer(k):
        return device(xl, yh, yl, c, h, (z + k) % 8)

    sends = []

    def send(src, dst, ss_, rs_, to):
        copy = pltpu.make_async_remote_copy(
            src_ref=src, dst_ref=dst, send_sem=ss_, recv_sem=rs_, device_id=to, device_id_type=MESH
        )
        copy.start()
        sends.append(copy)

    own_c = pltpu.make_async_copy(cot, cx.at[0], local_sem.at[0])
    own_c.start()
    own_p = pltpu.make_async_copy(p, pblk, local_sem.at[1])
    own_p.start()

    barrier = pltpu.get_barrier_semaphore()
    peers = [partner(0, i, kc) for i in range(4) for kc in range(2) if (i, kc) != (0, 0)]
    peers += [partner(1, i, kc) for i in range(1, 4) for kc in range(2)]
    peers += [z_peer(k) for k in range(1, 8)]
    for peer in peers:
        pl.semaphore_signal(barrier, inc=1, device_id=peer, device_id_type=MESH)

    odd = z % 2
    quarter = (1 - odd) * (xl * 2 + c) + odd * (yl * 2 + c)
    rows = pl.ds(pl.multiple_of(quarter * 128, 128), 128)
    foreign = odd * (h + yh - 2 * h * yh)

    def slot_of(zz):
        return (zz % 2) * 4 + zz // 2

    slot = slot_of(z)

    @pl.when(foreign == 0)
    def _():
        for n, (src, dst) in enumerate(((p, pg), (w, wg))):
            pltpu.make_async_copy(src.at[rows], dst.at[slot], local_sem.at[2 + n]).start()


    def columns(axis, i, kc, t):
        hi, lo = PAIRS[i]
        if axis == 0:
            q = flip(xl, lo) * 2 + flip(c, kc)
            block = flip(h, hi) * 8 + 2 * t
        else:
            q = flip(yl, lo) * 2 + flip(c, kc)
            block = flip(yh, hi) * 8 + 2 * t + 1
        return pl.ds(pl.multiple_of(block * 512 + q * 128, 128), 128)

    for axis in range(2):
        for t in range(4):
            pltpu.make_async_copy(
                inp.at[:, columns(axis, 0, 0, t)],
                xx.at[axis, 0, :, pl.ds(t * 128, 128)],
                local_sem.at[4 + axis],
            ).start()

    for n, ref in enumerate((m_in, v_in)):
        for half in range(2):
            mvz[z, n, half * 4 : half * 4 + 4, :] = ref[:, half * 512 : half * 512 + 512]

    pl.semaphore_wait(barrier, len(peers))

    own_c.wait()
    for axis in range(2):
        for i in ORDER:
            dst = (cx if axis == 0 else cy).at[2 * i]
            send(cx.at[0], dst, c_send.at[axis, i], c_recv.at[axis, i, 0], partner(axis, i, 0))
    send(cx.at[0], cx.at[1], c_send.at[0, 0], c_recv.at[0, 0, 1], partner(0, 0, 1))

    @pl.when(odd * (1 - foreign) == 1)
    def _():
        for n, (src, dst) in enumerate(((p, pg), (w, wg))):
            pltpu.make_async_remote_copy(
                src_ref=src.at[rows], dst_ref=dst.at[slot], send_sem=pre_send.at[n], recv_sem=pre_recv.at[n],
                device_id=partner(0, 3, 0), device_id_type=MESH,
            ).start()

    rings = (pg, wg)

    def ring_send(n, direction, t, a):
        sign = 1 if direction == 0 else -1
        piece = rings[n].at[slot_of((z - sign * (t - 1)) % 8), pl.ds(a * 64, 64)]
        index = (t - 1) * 2 + a
        send(piece, piece, ring_send_sem.at[n, direction, index], ring_recv_sem.at[n, direction, index], z_peer(sign))

    def ring_step(n, t):
        for a in range(2):
            for direction in range(2):
                if t == 4 and a != direction:
                    continue
                sign = 1 if direction == 0 else -1
                piece = rings[n].at[slot_of((z - sign * t) % 8), pl.ds(a * 64, 64)]
                wait_bytes(piece, ring_recv_sem.at[n, direction, (t - 1) * 2 + a])
                if t + 1 < 4 or (t + 1 == 4 and a == direction):
                    ring_send(n, direction, t + 1, a)

    def ring_start(n):
        @pl.when(foreign == 1)
        def _():
            wait_bytes(rings[n].at[slot], pre_recv.at[n])

        @pl.when(foreign == 0)
        def _():
            wait_bytes(rings[n].at[slot], local_sem.at[2 + n])

        for a in range(2):
            for direction in range(2):
                ring_send(n, direction, 1, a)

    ring_start(0)

    def send_inputs(axis, i, kc):
        for t in range(4):
            pltpu.make_async_remote_copy(
                src_ref=inp.at[:, columns(axis, i, kc, t)],
                dst_ref=xx.at[axis, 2 * i + kc, :, pl.ds(t * 128, 128)],
                send_sem=x_send.at[axis, 2 * i + kc],
                recv_sem=x_recv.at[axis, 2 * i + kc],
                device_id=partner(axis, i, kc),
                device_id_type=MESH,
            ).start()

    for i in ORDER:
        for kc in range(2):
            for axis in range(2):
                send_inputs(axis, i, kc)
    for axis in range(2):
        send_inputs(axis, 0, 1)

    for k in range(1, 8):
        send(mvz.at[z], mvz.at[z], mv_send.at[k - 1], mv_recv.at[k - 1], z_peer(k))

    def transpose_pair(pair, first, second):
        ct[pair, :, 0:128] = jnp.swapaxes(first, 0, 1)
        ct[pair, :, 128:256] = jnp.swapaxes(second, 0, 1)

    def take_cotangent(axis, i):
        ref = cx if axis == 0 else cy
        wait_bytes(ref.at[2 * i], c_recv.at[axis, i, 0])
        send(ref.at[2 * i], ref.at[2 * i + 1], e_send.at[axis, i], c_recv.at[axis, i, 1], partner(0, 0, 1))

    def turn_cotangent(axis, i):
        ref = cx if axis == 0 else cy
        wait_bytes(ref.at[2 * i + 1], c_recv.at[axis, i, 1])
        transpose_pair(axis * 3 + i, ref[2 * i], ref[2 * i + 1])

    def add_inputs(axis, i, first, last):
        if i == 0:
            wait_bytes(xx.at[axis, 0], local_sem.at[4 + axis])
            wait_bytes(xx.at[axis, 1], x_recv.at[axis, 1])
            pair = 0
        else:
            for kc in range(2):
                wait_bytes(xx.at[axis, 2 * i + kc], x_recv.at[axis, 2 * i + kc])
            pair = axis * 3 + i
        cols = pl.ds(axis * 512, 512)

        def body(r, carry):
            rs = pl.ds(pl.multiple_of(r * 256, 256), 256)
            x = xx[axis, 2 * i : 2 * i + 2].reshape(256, 512)
            part = dot(ct[pair, rs, :], x)
            if not first:
                part = part + mf[rs, cols]
            if last:
                mb[rs, cols] = part.astype(BF16)
            else:
                mf[rs, cols] = part
            return carry

        lax.fori_loop(0, 4, body, 0)

    wait_bytes(cx.at[1], c_recv.at[0, 0, 1])
    transpose_pair(0, cx[0], cx[1])
    ring_step(0, 1)
    for i in (1, 3):
        for axis in range(2):
            take_cotangent(axis, i)
    for i in (1, 3):
        for axis in range(2):
            turn_cotangent(axis, i)
    for axis in range(2):
        add_inputs(axis, 0, True, False)
    ring_step(0, 2)
    for axis in range(2):
        take_cotangent(axis, 2)
    for axis in range(2):
        turn_cotangent(axis, 2)
    for i in (1, 3):
        for axis in range(2):
            add_inputs(axis, i, False, False)
        if i == 1:
            ring_step(0, 3)
            ring_start(1)
    for axis in range(2):
        add_inputs(axis, 2, False, True)
    ring_step(0, 4)
    ring_step(1, 1)

    basis = pg[...].reshape(1024, 1024)

    def to_sibling(b, carry):
        rows_b = pl.ds(pl.multiple_of(b * 128 + (1 - c) * 64, 64), 64)
        s0[b] = dot(mb[rows_b, :], basis).astype(BF16)
        return carry

    def own_part(b, carry):
        rows_b = pl.ds(pl.multiple_of(b * 128 + c * 64, 64), 64)
        a_keep[b] = dot(mb[rows_b, :], basis)
        return carry

    for n in range(2):
        lax.fori_loop(n * 4, n * 4 + 4, to_sibling, 0)
        send(s0.at[n * 4 : n * 4 + 4], r0.at[n * 4 : n * 4 + 4], s_send.at[n], s_recv.at[n], partner(0, 0, 1))
    lax.fori_loop(0, 8, own_part, 0)
    for n in range(2):
        wait_bytes(r0.at[n * 4 : n * 4 + 4], s_recv.at[n])

    def add_sibling(b, carry):
        xl_, y_ = b // 4, b % 4
        for hh in range(2):
            rs = slice(hh * 32, hh * 32 + 32)
            total = a_keep[b, rs, :] + r0[b, rs, :].astype(F32)
            a0[hh, xl_, y_] = total[:, 0:512].astype(BF16)
            a1[y_, xl_, hh] = total[:, 512:1024].astype(BF16)
        return carry

    lax.fori_loop(0, 8, add_sibling, 0)

    for i in ORDER:
        hi, lo = PAIRS[i]
        send(a0.at[flip(h, hi), flip(xl, lo)], ra0.at[i - 1], a_send.at[0, i - 1], a_recv.at[0, i - 1], partner(0, i, 0))
        send(a1.at[flip(yh, hi) * 2 + flip(yl, lo)], ra1.at[i - 1], a_send.at[1, i - 1], a_recv.at[1, i - 1], partner(1, i, 0))
    ring_step(1, 2)
    for n, ref in enumerate((ra0, ra1)):
        for i in range(3):
            wait_bytes(ref.at[i], a_recv.at[n, i])
    b0[...] = (a0[h, xl].astype(F32) + ra0[0].astype(F32) + ra0[1].astype(F32) + ra0[2].astype(F32)).astype(BF16)
    b1[...] = (a1[y].astype(F32) + ra1[0].astype(F32) + ra1[1].astype(F32) + ra1[2].astype(F32)).astype(BF16)
    for i in ORDER:
        hi, lo = PAIRS[i]
        send(b0.at[flip(yh, hi) * 2 + flip(yl, lo)], rb0.at[i - 1], b_send.at[0, i - 1], b_recv.at[0, i - 1], partner(1, i, 0))
        send(b1.at[flip(xl, lo), flip(h, hi)], rb1.at[i - 1], b_send.at[1, i - 1], b_recv.at[1, i - 1], partner(0, i, 0))
    for n, ref in enumerate((rb0, rb1)):
        for i in range(3):
            wait_bytes(ref.at[i], b_recv.at[n, i])
    f0 = b0[y].astype(F32) + rb0[0].astype(F32) + rb0[1].astype(F32) + rb0[2].astype(F32)
    f1 = b1[xl, h].astype(F32) + rb1[0].astype(F32) + rb1[1].astype(F32) + rb1[2].astype(F32)
    for zz in range(8):
        cs[zz, 0:4, :] = f0[zz * 4 : zz * 4 + 4]
        cs[zz, 4:8, :] = f1[zz * 4 : zz * 4 + 4]
    for k in range(1, 8):
        send(cs.at[(z + k) % 8], rc.at[k - 1], z_send.at[k - 1], z_recv.at[k - 1], z_peer(k))
    g = cs[z]
    for k in range(1, 8):
        wait_bytes(rc.at[k - 1], z_recv.at[k - 1])
        g = g + rc[k - 1]
    gz[z] = g
    for k in range(1, 8):
        send(gz.at[z], gz.at[z], g_send.at[k - 1], g_recv.at[k - 1], z_peer(k))
    for k in range(1, 8):
        wait_bytes(gz.at[(z - k) % 8], g_recv.at[k - 1])
        wait_bytes(mvz.at[(z - k) % 8], mv_recv.at[k - 1])

    squares = jnp.sum(gz[...] * gz[...])
    ss[0] = jnp.full((8, 128), squares, F32)
    for i in range(4):
        for kc in range(2):
            k = 2 * i + kc
            if k:
                send(ss.at[0], sr_a.at[k - 1], q_send.at[k - 1], q_recv.at[k - 1], partner(0, i, kc))
    total = ss[0]
    for k in range(1, 8):
        wait_bytes(sr_a.at[k - 1], q_recv.at[k - 1])
        total = total + sr_a[k - 1]
    ss[1] = total
    for i in range(1, 4):
        send(ss.at[1], sr_b.at[i - 1], q_send.at[6 + i], q_recv.at[6 + i], partner(1, i, 0))
    for i in range(1, 4):
        wait_bytes(sr_b.at[i - 1], q_recv.at[6 + i])
        total = total + sr_b[i - 1]
    factor = jnp.minimum(1.0, lax.rsqrt(total * (1.0 / ENTRIES) + 1e-06))[0:1, 0:1]

    def adam(gradient, first, second):
        clipped = gradient * factor
        new_first = beta_one * first + (1.0 - beta_one) * clipped
        new_second = beta_two * second + (1.0 - beta_two) * clipped * clipped
        return new_first, new_second

    for zz in range(8):
        first, second = adam(gz[zz], mvz[zz, 0], mvz[zz, 1])
        direction = first / bias_one / (jnp.sqrt(second / bias_two) + 1e-08)
        df[zz * 4 : zz * 4 + 4, 0:512] = direction[0:4]
        df[zz * 4 : zz * 4 + 4, 512:1024] = direction[4:8]
    dall[xl, y, c, h] = df[...].astype(BF16)

    halves = (pl.ds(0, 512), pl.ds(512, 512))
    own = dall.at[xl, y, c, h]
    for i in ORDER:
        for axis in range(2):
            piece = dall.at[xl, y, c, h, :, halves[axis]]
            send(piece, piece, d_send.at[0, axis, i - 1], d_recv.at[0, axis, i - 1], partner(axis, i, 0))

    first, second = adam(gz[z], mvz[z, 0], mvz[z, 1])
    for half in range(2):
        nf[:, half * 512 : half * 512 + 512] = first[half * 4 : half * 4 + 4]
        nv[:, half * 512 : half * 512 + 512] = second[half * 4 : half * 4 + 4]

    for i in ORDER:
        hi, lo = PAIRS[i]
        wait_bytes(dall.at[flip(xl, lo), y, c, flip(h, hi), :, halves[0]], d_recv.at[0, 0, i - 1])
        wait_bytes(dall.at[xl, flip(yh, hi) * 2 + flip(yl, lo), c, h, :, halves[1]], d_recv.at[0, 1, i - 1])
    along_x = lambda y_, c_: dall.at[:, y_, c_, :, :, halves[0]]
    along_y = lambda xl_, h_, c_: dall.at[xl_, :, c_, h_, :, halves[1]]
    for i in ORDER:
        send(along_x(y, c), along_x(y, c), d_send.at[1, 0, i - 1], d_recv.at[1, 0, i - 1], partner(1, i, 0))
        send(along_y(xl, h, c), along_y(xl, h, c), d_send.at[1, 1, i - 1], d_recv.at[1, 1, i - 1], partner(0, i, 0))
    send(along_x(y, c), along_x(y, c), e_send.at[2, 0], e_recv.at[0, 0], partner(0, 0, 1))
    send(along_y(xl, h, c), along_y(xl, h, c), e_send.at[3, 0], e_recv.at[1, 0], partner(0, 0, 1))
    ring_step(1, 3)
    for i in ORDER:
        hi, lo = PAIRS[i]
        y_ = flip(yh, hi) * 2 + flip(yl, lo)
        wait_bytes(along_x(y_, c), d_recv.at[1, 0, i - 1])
        send(along_x(y_, c), along_x(y_, c), e_send.at[2, i], e_recv.at[0, i], partner(0, 0, 1))
        xl_, h_ = flip(xl, lo), flip(h, hi)
        wait_bytes(along_y(xl_, h_, c), d_recv.at[1, 1, i - 1])
        send(along_y(xl_, h_, c), along_y(xl_, h_, c), e_send.at[3, i], e_recv.at[1, i], partner(0, 0, 1))

    ring_step(1, 4)
    for axis in range(2):
        for i in ORDER + (0,):
            ref = cy if axis == 1 and i > 0 else cx
            a = ref[2 * i : 2 * i + 2].reshape(256, 1024)
            b = wg[axis * 4 : axis * 4 + 4].reshape(512, 1024)
            igb[axis, 2 * i : 2 * i + 2] = dot(a, b, NT).astype(BF16).reshape(2, 128, 512)
            for kc in range(2):
                k = 2 * i + kc
                for t in range(4):
                    src = igb.at[axis, k, :, pl.ds(t * 128, 128)]
                    dst = ig.at[:, columns(axis, 0, 0, t)]
                    if k == 0:
                        pltpu.make_async_copy(src, dst, local_sem.at[6 + axis]).start()
                    else:
                        pltpu.make_async_remote_copy(
                            src_ref=src, dst_ref=dst, send_sem=o_send.at[axis, k], recv_sem=o_recv.at[axis, k],
                            device_id=partner(axis, i, kc), device_id_type=MESH,
                        ).start()

    for i in range(4):
        hi, lo = PAIRS[i]
        y_ = flip(yh, hi) * 2 + flip(yl, lo)
        wait_bytes(along_x(y_, 1 - c), e_recv.at[0, i])
        wait_bytes(along_y(flip(xl, lo), flip(h, hi), 1 - c), e_recv.at[1, i])
    own_p.wait()
    for n in range(4):
        xl_, y0 = n // 2, (n % 2) * 2
        rows_d = dall[xl_, y0 : y0 + 2].reshape(256, 1024)
        wu[:, n * 256 : n * 256 + 256] = dot(pblk[...], rows_d, NT).astype(BF16)

    for axis in range(2):
        wait_bytes(igb.at[axis, 0], local_sem.at[6 + axis])
        for k in range(1, 8):
            wait_bytes(xx.at[axis, k], x_send.at[axis, k])
            wait_bytes(igb.at[axis, k], o_send.at[axis, k])
            wait_bytes(igb.at[axis, k], o_recv.at[axis, k])

    @pl.when(odd * (1 - foreign) == 1)
    def _():
        for n in range(2):
            wait_bytes(rings[n].at[slot], pre_send.at[n])

    for copy in sends:
        copy.wait_send()


def local(inputs, cotangent, weight, projector, first_moment_state, second_moment_state):
    anywhere = pl.BlockSpec(memory_space=pl.ANY)
    vmem = pl.BlockSpec(memory_space=pltpu.VMEM)
    dma = pltpu.SemaphoreType.DMA
    V = pltpu.VMEM
    return pl.pallas_call(
        kernel,
        out_shape=(
            jax.ShapeDtypeStruct((TOKENS, WIDTH), BF16),
            jax.ShapeDtypeStruct((512, OUTS), BF16),
            jax.ShapeDtypeStruct((4, RANK), F32),
            jax.ShapeDtypeStruct((4, RANK), F32),
        ),
        in_specs=[anywhere] * 4 + [vmem] * 2,
        out_specs=(anywhere, vmem, vmem, vmem),
        scratch_shapes=[
            V((8, 128, 1024), BF16),
            V((8, 128, 1024), BF16),
            V((7, 1024, 256), BF16),
            V((2, 8, 128, 512), BF16),
            V((8, 128, 1024), BF16),
            V((8, 128, 1024), BF16),
            V((512, 1024), BF16),
            V((1024, 1024), F32),
            V((1024, 1024), BF16),
            V((2, 8, 128, 512), BF16),
            V((8, 64, 1024), BF16),
            V((8, 64, 1024), BF16),
            V((8, 64, 1024), F32),
            V((2, 2, 4, 32, 512), BF16),
            V((4, 2, 2, 32, 512), BF16),
            V((3, 4, 32, 512), BF16),
            V((3, 2, 2, 32, 512), BF16),
            V((4, 32, 512), BF16),
            V((2, 2, 32, 512), BF16),
            V((3, 32, 512), BF16),
            V((3, 32, 512), BF16),
            V((8, 8, 512), F32),
            V((7, 8, 512), F32),
            V((8, 8, 512), F32),
            V((8, 2, 8, 512), F32),
            V((2, 8, 128), F32),
            V((7, 8, 128), F32),
            V((3, 8, 128), F32),
            V((32, 1024), F32),
            V((2, 4, 2, 2, 32, 1024), BF16),
            dma((8,)),
            dma((2, 4)), dma((2, 4, 2)),
            dma((2, 8)), dma((2, 8)),
            dma((2,)), dma((2,)),
            dma((2, 2, 8)), dma((2, 2, 8)),
            dma((7,)), dma((7,)),
            dma((2, 8)), dma((2, 8)),
            dma((2,)), dma((2,)),
            dma((2, 3)), dma((2, 3)),
            dma((2, 3)), dma((2, 3)),
            dma((7,)), dma((7,)),
            dma((7,)), dma((7,)),
            dma((10,)), dma((10,)),
            dma((2, 2, 3)), dma((2, 2, 3)),
            dma((4, 4)), dma((2, 4)),
        ],
        compiler_params=pltpu.CompilerParams(
            collective_id=0, has_side_effects=True, vmem_limit_bytes=56 << 20
        ),
        name="galore",
    )(inputs, cotangent, weight, projector, first_moment_state, second_moment_state)


def solution(mesh):
    return jax.shard_map(
        local,
        mesh=mesh,
        in_specs=(
            P(("dp", "shard"), None),
            P(("dp", "shard"), None),
            P("shard", None),
            P("shard", None),
            P(("dp", "shard"), None),
            P(("dp", "shard"), None),
        ),
        out_specs=(
            P(("dp", "shard"), None),
            P("shard", None),
            P(("dp", "shard"), None),
            P(("dp", "shard"), None),
        ),
        check_vma=False,
    )
```

time: 1580 us -> 140 us (0.09)
  waiting for transfers between devices: 1390 us -> 0 us
  blocking collectives: 138 us -> 0 us
  Pallas kernels: 0 us -> 133 us
  matrix products: 24.5 us -> 0 us
    all_gather x2 -> x0, waiting for transfers between devices: 910 us -> none  [the longest x1 691 us: local(): lax.all_gather(direction, ('dp', 'shard'), axis=0, tiled=True)]
    unnamed x5 -> x0, waiting for transfers between devices: 273 us -> none
    reduce_scatter x1 -> x0, waiting for transfers between devices: 203 us -> none  [local(): lax.psum_scatter(lax.optimization_barrier(part_term.astype(jnp.bfloat16))...]
    pallas_call x0 -> x1, Pallas kernels: none -> 133 us  [local(): pl.pallas_call(kernel, out_shape=(jax.ShapeDtypeStruct((TOKENS, WIDTH), B...]
    psum x1 -> x0, blocking collectives: 77.7 us -> none  [local(): lax.psum(jnp.sum(key_gradient * key_gradient), ('dp', 'shard'))]
    all_to_all x1 -> x0, blocking collectives: 60.5 us -> none  [local(): lax.all_to_all(inputs, 'shard', split_axis=1, concat_axis=0, tiled=True)]
    dot_general x4 -> x0, matrix products: 24.5 us -> none  [the longest x1 12.7 us: local(): lax.dot_general(cotangent, lax.all_gather(weight, 'shard', axis=0, tiled=...]
  transfers between devices with their start and end apart: 4 -> 0, of which waited for: 4 -> 0; matrix products, arithmetic and copies ran while one was open for 0% -> 0% of each run, Pallas kernels for 0% -> 0%
where the time goes in v1:
time: 140 us; the launch traced here: 139 us
  Pallas kernels  133 us (95%)
  local copies, waits for them, and re-layouts  5.37 us (4%)
    pallas_call x1, Pallas kernels, local(): pl.pallas_call(kernel, out_shape=(jax.ShapeDtypeStruct((TOKENS, WIDTH), B...  133 us
    unnamed x10, local copies, waits for them, and re-layouts  5.37 us

profile of v1, /device:TPU:1, one launch (start us, length us, event | category | flops | bytes accessed | tf_op | source)
XLA Modules:
  0.0 139.3 jit_solution(9975685852142117533)
XLA Ops:
  0.6 133.3 %galore.1 = (bf16[128,8192]{1,0:T(8,128)(2,1)}, bf16[512,1024]{1,0:T(8,128)(2,1)}, f32[4,1024]{1,0:T(4,128)}, f32[4,1024]{1,0:T(4,128)}) custom-call(bf16[128,8192]{1,0:T(8,128)(2,1)} %inp.1, bf16[128,1024]{1,0:T(8,128)(2,1)} %cot.1, bf16[512,1024]{1,0:T(8,128)(2,1)} %w.1, bf16[512,1024]{1,0:T(8,128)(2,1)} %p.1, f32[4,1024]{1,0:T(4,128)} %m_in.1, f32[4,1024]{1,0:T(4,128)} %v_in.1), custom_call_target="tpu_custom_call" | custom-call | tf_op jit(solution)/shard_map/galore/pallas_call | solution.py:454
  133.9 0.0 copy-start
  133.9 0.0 copy-start.2
  133.9 3.2 %copy.14 = bf16[128,8192]{1,0:T(8,128)(2,1)} copy(bf16[128,8192]{1,0:T(8,128)(2,1)} %get-tuple-element.8) | data formatting | bytes 4194304
  137.1 0.0 copy-done
  137.1 0.0 copy-start.1
  137.1 1.0 copy.15
  138.1 0.0 copy-done.2
  138.1 0.6 copy.16
  138.7 0.0 copy-done.1
  138.7 0.6 copy.17
Async XLA Ops:
  133.9 3.2 %copy-start = (bf16[512,1024]{1,0:T(8,128)(2,1)S(1)}, bf16[512,1024]{1,0:T(8,128)(2,1)}, u32[]{:S(2)}) copy-start(bf16[512,1024]{1,0:T(8,128)(2,1)} %get-tuple-element.9) | copy-start | bytes 3145732
  133.9 4.2 %copy-start.2 = (f32[4,1024]{1,0:T(4,128)S(1)}, f32[4,1024]{1,0:T(4,128)}, u32[]{:S(2)}) copy-start(f32[4,1024]{1,0:T(4,128)} %get-tuple-element.10) | copy-start | bytes 49156
  137.1 1.6 %copy-start.1 = (f32[4,1024]{1,0:T(4,128)S(1)}, f32[4,1024]{1,0:T(4,128)}, u32[]{:S(2)}) copy-start(f32[4,1024]{1,0:T(4,128)} %get-tuple-element.11) | copy-start | bytes 49156

commit v2 on v1

--- a/solution.py
+++ b/solution.py
@@ -22,6 +22,7 @@
 
 NN = (((1,), (0,)), ((), ()))
 NT = (((1,), (1,)), ((), ()))
+TN = (((0,), (0,)), ((), ()))
 
 
 def dot(a, b, dims=NN):
@@ -43,12 +44,12 @@
 def kernel(
     inp, cot, w, p, m_in, v_in,
     ig, wu, nf, nv,
-    cx, cy, ct, xx, pg, wg, pblk, mf, mb, igb,
+    cx, cy, xx, pg, wg, pblk, mf, mb, igb,
     s0, r0, a_keep, a0, a1, ra0, ra1, b0, b1, rb0, rb1, cs, rc, gz, mvz, ss, sr_a, sr_b, df, dall,
     local_sem, c_send, c_recv, x_send, x_recv, pre_send, pre_recv,
     ring_send_sem, ring_recv_sem, mv_send, mv_recv, o_send, o_recv,
     s_send, s_recv, a_send, a_recv, b_send, b_recv, z_send, z_recv, g_send, g_recv,
-    q_send, q_recv, d_send, d_recv, e_send, e_recv,
+    q_send, q_recv, d_send, d_recv, e_send, e_recv, f_send, f_recv,
 ):
     d = lax.axis_index("dp")
     s = lax.axis_index("shard")
@@ -95,19 +96,26 @@
 
     odd = z % 2
     quarter = (1 - odd) * (xl * 2 + c) + odd * (yl * 2 + c)
-    rows = pl.ds(pl.multiple_of(quarter * 128, 128), 128)
     foreign = odd * (h + yh - 2 * h * yh)
 
     def slot_of(zz):
         return (zz % 2) * 4 + zz // 2
 
     slot = slot_of(z)
+
+    def half_rows(half):
+        return pl.ds(pl.multiple_of(quarter * 128 + half * 64, 64), 64)
+
+    def shared(t):
+        e = (odd + t) % 2
+        half = (1 - e) * yl + e * xl
+        return half, device(xl + e * (1 - 2 * xl), yh, yl + (1 - e) * (1 - 2 * yl), c, h, z)
 
     @pl.when(foreign == 0)
     def _():
         for n, (src, dst) in enumerate(((p, pg), (w, wg))):
-            pltpu.make_async_copy(src.at[rows], dst.at[slot], local_sem.at[2 + n]).start()
-
+            for half in range(2):
+                pltpu.make_async_copy(src.at[half_rows(half)], dst.at[slot, half], local_sem.at[2 + n]).start()
 
     def columns(axis, i, kc, t):
         hi, lo = PAIRS[i]
@@ -133,54 +141,87 @@
 
     pl.semaphore_wait(barrier, len(peers))
 
-    own_c.wait()
-    for axis in range(2):
-        for i in ORDER:
-            dst = (cx if axis == 0 else cy).at[2 * i]
-            send(cx.at[0], dst, c_send.at[axis, i], c_recv.at[axis, i, 0], partner(axis, i, 0))
-    send(cx.at[0], cx.at[1], c_send.at[0, 0], c_recv.at[0, 0, 1], partner(0, 0, 1))
-
-    @pl.when(odd * (1 - foreign) == 1)
-    def _():
-        for n, (src, dst) in enumerate(((p, pg), (w, wg))):
-            pltpu.make_async_remote_copy(
-                src_ref=src.at[rows], dst_ref=dst.at[slot], send_sem=pre_send.at[n], recv_sem=pre_recv.at[n],
-                device_id=partner(0, 3, 0), device_id_type=MESH,
-            ).start()
-
+    def cross(n, src, dst):
+        @pl.when(odd * (1 - foreign) == 1)
+        def _():
+            for a in range(2) if n == 0 else (1 - xl,):
+                pltpu.make_async_remote_copy(
+                    src_ref=src.at[half_rows(a)], dst_ref=dst.at[slot, a],
+                    send_sem=pre_send.at[n], recv_sem=pre_recv.at[n],
+                    device_id=partner(0, 3, 0), device_id_type=MESH,
+                ).start()
+
+    cross(0, p, pg)
     rings = (pg, wg)
 
-    def ring_send(n, direction, t, a):
-        sign = 1 if direction == 0 else -1
-        piece = rings[n].at[slot_of((z - sign * (t - 1)) % 8), pl.ds(a * 64, 64)]
+    def ring_piece(n, direction, t, a):
+        piece = rings[n].at[slot_of((z - (1 if direction == 0 else -1) * t) % 8)]
+        return piece.at[a] if n == 0 else piece.at[shared(t)[0], pl.ds(a * 32, 32)]
+
+    def ring_copy(n, direction, t, a):
+        piece = ring_piece(n, direction, t - 1, a)
         index = (t - 1) * 2 + a
-        send(piece, piece, ring_send_sem.at[n, direction, index], ring_recv_sem.at[n, direction, index], z_peer(sign))
+        return pltpu.make_async_remote_copy(
+            src_ref=piece, dst_ref=piece,
+            send_sem=ring_send_sem.at[n, direction, index], recv_sem=ring_recv_sem.at[n, direction, index],
+            device_id=z_peer(1 if direction == 0 else -1), device_id_type=MESH,
+        )
+
+    def neighbour_half(direction, t, other):
+        half = shared(t)[0]
+        return wg.at[slot_of((z - (1 if direction == 0 else -1) * t) % 8), 1 - half if other else half]
+
+    def hand_over(direction, t, index):
+        piece = neighbour_half(direction, t, False)
+        send(piece, piece, f_send.at[index], f_recv.at[index], shared(t)[1])
 
     def ring_step(n, t):
         for a in range(2):
             for direction in range(2):
                 if t == 4 and a != direction:
                     continue
-                sign = 1 if direction == 0 else -1
-                piece = rings[n].at[slot_of((z - sign * t) % 8), pl.ds(a * 64, 64)]
-                wait_bytes(piece, ring_recv_sem.at[n, direction, (t - 1) * 2 + a])
+                wait_bytes(ring_piece(n, direction, t, a), ring_recv_sem.at[n, direction, (t - 1) * 2 + a])
                 if t + 1 < 4 or (t + 1 == 4 and a == direction):
-                    ring_send(n, direction, t + 1, a)
-
-    def ring_start(n):
+                    onward = ring_copy(n, direction, t + 1, a)
+                    onward.start()
+                    sends.append(onward)
+        for direction in range((2 if t < 4 else 1) if n == 1 else 0):
+            hand_over(direction, t, (t - 1) * 2 + direction)
+
+    def ring_start(n, which):
+        @pl.when(foreign == which)
+        def _():
+            if which:
+                wait_bytes(rings[n].at[slot] if n == 0 else rings[n].at[slot, xl], pre_recv.at[n])
+                if n == 1:
+                    own_half().start()
+            else:
+                wait_bytes(rings[n].at[slot], local_sem.at[2 + n])
+            for a in range(2):
+                for direction in range(2):
+                    ring_copy(n, direction, 1, a).start()
+
+        if which:
+            sends.extend(ring_copy(n, direction, 1, a) for a in range(2) for direction in range(2))
+
+    def own_half():
+        piece = wg.at[slot, xl]
+        return pltpu.make_async_remote_copy(
+            src_ref=piece, dst_ref=piece, send_sem=f_send.at[7], recv_sem=f_recv.at[7],
+            device_id=partner(0, 1, 0), device_id_type=MESH,
+        )
+
+    def ring_end():
+        for t in range(1, 5):
+            for direction in range(2 if t < 4 else 1):
+                wait_bytes(neighbour_half(direction, t, True), f_recv.at[(t - 1) * 2 + direction])
+
         @pl.when(foreign == 1)
         def _():
-            wait_bytes(rings[n].at[slot], pre_recv.at[n])
-
-        @pl.when(foreign == 0)
-        def _():
-            wait_bytes(rings[n].at[slot], local_sem.at[2 + n])
-
-        for a in range(2):
-            for direction in range(2):
-                ring_send(n, direction, 1, a)
-
-    ring_start(0)
+            wait_bytes(wg.at[slot, 1 - xl], f_recv.at[7])
+            wait_bytes(wg.at[slot, xl], f_send.at[7])
+
+    ring_start(0, 0)
 
     def send_inputs(axis, i, kc):
         for t in range(4):
@@ -193,117 +234,125 @@
                 device_id_type=MESH,
             ).start()
 
-    for i in ORDER:
-        for kc in range(2):
-            for axis in range(2):
+    own_c.wait()
+    send(cx.at[0], cx.at[1], c_send.at[0, 0], c_recv.at[0, 0, 1], partner(0, 0, 1))
+    for axis in (1, 0):
+        if axis == 0:
+            @pl.when(odd * (1 - foreign) == 1)
+            def _():
+                wait_bytes(pg.at[slot], pre_send.at[0])
+
+        for i in ORDER:
+            dst = (cx if axis == 0 else cy).at[2 * i]
+            send(cx.at[0], dst, c_send.at[axis, i], c_recv.at[axis, i, 0], partner(axis, i, 0))
+        for i in ORDER:
+            for kc in range(2):
                 send_inputs(axis, i, kc)
-    for axis in range(2):
         send_inputs(axis, 0, 1)
 
-    for k in range(1, 8):
-        send(mvz.at[z], mvz.at[z], mv_send.at[k - 1], mv_recv.at[k - 1], z_peer(k))
-
-    def transpose_pair(pair, first, second):
-        ct[pair, :, 0:128] = jnp.swapaxes(first, 0, 1)
-        ct[pair, :, 128:256] = jnp.swapaxes(second, 0, 1)
+    ring_start(0, 1)
+    cross(1, w, wg)
 
     def take_cotangent(axis, i):
         ref = cx if axis == 0 else cy
         wait_bytes(ref.at[2 * i], c_recv.at[axis, i, 0])
         send(ref.at[2 * i], ref.at[2 * i + 1], e_send.at[axis, i], c_recv.at[axis, i, 1], partner(0, 0, 1))
 
-    def turn_cotangent(axis, i):
-        ref = cx if axis == 0 else cy
-        wait_bytes(ref.at[2 * i + 1], c_recv.at[axis, i, 1])
-        transpose_pair(axis * 3 + i, ref[2 * i], ref[2 * i + 1])
+    def pair_of(axis, i):
+        return (cy if axis == 1 and i > 0 else cx), slice(2 * i, 2 * i + 2)
 
     def add_inputs(axis, i, first, last):
+        ref, pair = pair_of(axis, i)
         if i == 0:
             wait_bytes(xx.at[axis, 0], local_sem.at[4 + axis])
             wait_bytes(xx.at[axis, 1], x_recv.at[axis, 1])
-            pair = 0
         else:
+            wait_bytes(ref.at[2 * i + 1], c_recv.at[axis, i, 1])
             for kc in range(2):
                 wait_bytes(xx.at[axis, 2 * i + kc], x_recv.at[axis, 2 * i + kc])
-            pair = axis * 3 + i
-        cols = pl.ds(axis * 512, 512)
-
-        def body(r, carry):
-            rs = pl.ds(pl.multiple_of(r * 256, 256), 256)
-            x = xx[axis, 2 * i : 2 * i + 2].reshape(256, 512)
-            part = dot(ct[pair, rs, :], x)
+        cols = slice(axis * 512, axis * 512 + 512)
+        x = xx[axis, pair].reshape(256, 512)
+        for r in range(4):
+            rs = slice(r * 256, r * 256 + 256)
+            part = dot(ref[pair, :, rs].reshape(256, 256), x, TN)
             if not first:
                 part = part + mf[rs, cols]
             if last:
-                mb[rs, cols] = part.astype(BF16)
+                part = part.astype(BF16).reshape(2, 2, 64, 512)
+                for core in range(2):
+                    mb[core, 2 * r : 2 * r + 2, :, cols] = part[:, core]
             else:
                 mf[rs, cols] = part
-            return carry
-
-        lax.fori_loop(0, 4, body, 0)
-
+
+    ring_step(0, 1)
+    ring_step(0, 2)
+    for axis in (1, 0):
+        for i in (1, 3):
+            take_cotangent(axis, i)
+    ring_step(0, 3)
+    ring_start(1, 0)
+    ring_start(1, 1)
+    ring_step(0, 4)
+    for axis in (1, 0):
+        take_cotangent(axis, 2)
     wait_bytes(cx.at[1], c_recv.at[0, 0, 1])
-    transpose_pair(0, cx[0], cx[1])
-    ring_step(0, 1)
-    for i in (1, 3):
-        for axis in range(2):
-            take_cotangent(axis, i)
-    for i in (1, 3):
-        for axis in range(2):
-            turn_cotangent(axis, i)
-    for axis in range(2):
+    for axis in (1, 0):
         add_inputs(axis, 0, True, False)
-    ring_step(0, 2)
-    for axis in range(2):
-        take_cotangent(axis, 2)
-    for axis in range(2):
-        turn_cotangent(axis, 2)
-    for i in (1, 3):
-        for axis in range(2):
-            add_inputs(axis, i, False, False)
-        if i == 1:
-            ring_step(0, 3)
-            ring_start(1)
-    for axis in range(2):
-        add_inputs(axis, 2, False, True)
-    ring_step(0, 4)
     ring_step(1, 1)
+    for i in (1, 3, 2):
+        for axis in (1, 0):
+            add_inputs(axis, i, False, i == 2)
+
+    returns = [(axis, i) for i in ORDER + (0,) for axis in range(2)]
+
+    def return_gradient(first, last):
+        for axis, i in returns[first:last]:
+            ref, pair = pair_of(axis, i)
+            a = ref[pair].reshape(256, 1024)
+            b = wg[axis * 4 : axis * 4 + 4].reshape(512, 1024)
+            igb[axis, pair] = dot(a, b, NT).astype(BF16).reshape(2, 128, 512)
+            for kc in range(2):
+                k = 2 * i + kc
+                for t in range(4):
+                    src = igb.at[axis, k, :, pl.ds(t * 128, 128)]
+                    dst = ig.at[:, columns(axis, 0, 0, t)]
+                    if k == 0:
+                        pltpu.make_async_copy(src, dst, local_sem.at[6 + axis]).start()
+                    else:
+                        pltpu.make_async_remote_copy(
+                            src_ref=src, dst_ref=dst, send_sem=o_send.at[axis, k], recv_sem=o_recv.at[axis, k],
+                            device_id=partner(axis, i, kc), device_id_type=MESH,
+                        ).start()
 
     basis = pg[...].reshape(1024, 1024)
 
-    def to_sibling(b, carry):
-        rows_b = pl.ds(pl.multiple_of(b * 128 + (1 - c) * 64, 64), 64)
-        s0[b] = dot(mb[rows_b, :], basis).astype(BF16)
-        return carry
-
-    def own_part(b, carry):
-        rows_b = pl.ds(pl.multiple_of(b * 128 + c * 64, 64), 64)
-        a_keep[b] = dot(mb[rows_b, :], basis)
-        return carry
-
     for n in range(2):
-        lax.fori_loop(n * 4, n * 4 + 4, to_sibling, 0)
-        send(s0.at[n * 4 : n * 4 + 4], r0.at[n * 4 : n * 4 + 4], s_send.at[n], s_recv.at[n], partner(0, 0, 1))
-    lax.fori_loop(0, 8, own_part, 0)
+        group = slice(n * 4, n * 4 + 4)
+        s0[group] = dot(mb[1 - c, group].reshape(256, 1024), basis).astype(BF16).reshape(4, 64, 1024)
+        send(s0.at[group], r0.at[group], s_send.at[n], s_recv.at[n], partner(0, 0, 1))
+    ring_step(1, 2)
+    for n in range(2):
+        group = slice(n * 4, n * 4 + 4)
+        a_keep[group] = dot(mb[c, group].reshape(256, 1024), basis).reshape(4, 64, 1024)
+    ring_step(1, 3)
     for n in range(2):
         wait_bytes(r0.at[n * 4 : n * 4 + 4], s_recv.at[n])
 
-    def add_sibling(b, carry):
+    for b in range(8):
         xl_, y_ = b // 4, b % 4
+        total = a_keep[b] + r0[b].astype(F32)
         for hh in range(2):
             rs = slice(hh * 32, hh * 32 + 32)
-            total = a_keep[b, rs, :] + r0[b, rs, :].astype(F32)
-            a0[hh, xl_, y_] = total[:, 0:512].astype(BF16)
-            a1[y_, xl_, hh] = total[:, 512:1024].astype(BF16)
-        return carry
-
-    lax.fori_loop(0, 8, add_sibling, 0)
+            a0[hh, xl_, y_] = total[rs, 0:512].astype(BF16)
+            a1[y_, xl_, hh] = total[rs, 512:1024].astype(BF16)
 
     for i in ORDER:
         hi, lo = PAIRS[i]
         send(a0.at[flip(h, hi), flip(xl, lo)], ra0.at[i - 1], a_send.at[0, i - 1], a_recv.at[0, i - 1], partner(0, i, 0))
         send(a1.at[flip(yh, hi) * 2 + flip(yl, lo)], ra1.at[i - 1], a_send.at[1, i - 1], a_recv.at[1, i - 1], partner(1, i, 0))
-    ring_step(1, 2)
+    ring_step(1, 4)
+    for k in range(1, 8):
+        send(mvz.at[z], mvz.at[z], mv_send.at[k - 1], mv_recv.at[k - 1], z_peer(k))
     for n, ref in enumerate((ra0, ra1)):
         for i in range(3):
             wait_bytes(ref.at[i], a_recv.at[n, i])
@@ -323,6 +372,8 @@
         cs[zz, 4:8, :] = f1[zz * 4 : zz * 4 + 4]
     for k in range(1, 8):
         send(cs.at[(z + k) % 8], rc.at[k - 1], z_send.at[k - 1], z_recv.at[k - 1], z_peer(k))
+    ring_end()
+    return_gradient(0, 3)
     g = cs[z]
     for k in range(1, 8):
         wait_bytes(rc.at[k - 1], z_recv.at[k - 1])
@@ -330,6 +381,7 @@
     gz[z] = g
     for k in range(1, 8):
         send(gz.at[z], gz.at[z], g_send.at[k - 1], g_recv.at[k - 1], z_peer(k))
+    return_gradient(3, 6)
     for k in range(1, 8):
         wait_bytes(gz.at[(z - k) % 8], g_recv.at[k - 1])
         wait_bytes(mvz.at[(z - k) % 8], mv_recv.at[k - 1])
@@ -341,6 +393,7 @@
             k = 2 * i + kc
             if k:
                 send(ss.at[0], sr_a.at[k - 1], q_send.at[k - 1], q_recv.at[k - 1], partner(0, i, kc))
+    return_gradient(6, 8)
     total = ss[0]
     for k in range(1, 8):
         wait_bytes(sr_a.at[k - 1], q_recv.at[k - 1])
@@ -389,7 +442,6 @@
         send(along_y(xl, h, c), along_y(xl, h, c), d_send.at[1, 1, i - 1], d_recv.at[1, 1, i - 1], partner(0, i, 0))
     send(along_x(y, c), along_x(y, c), e_send.at[2, 0], e_recv.at[0, 0], partner(0, 0, 1))
     send(along_y(xl, h, c), along_y(xl, h, c), e_send.at[3, 0], e_recv.at[1, 0], partner(0, 0, 1))
-    ring_step(1, 3)
     for i in ORDER:
         hi, lo = PAIRS[i]
         y_ = flip(yh, hi) * 2 + flip(yl, lo)
@@ -398,26 +450,6 @@
         xl_, h_ = flip(xl, lo), flip(h, hi)
         wait_bytes(along_y(xl_, h_, c), d_recv.at[1, 1, i - 1])
         send(along_y(xl_, h_, c), along_y(xl_, h_, c), e_send.at[3, i], e_recv.at[1, i], partner(0, 0, 1))
-
-    ring_step(1, 4)
-    for axis in range(2):
-        for i in ORDER + (0,):
-            ref = cy if axis == 1 and i > 0 else cx
-            a = ref[2 * i : 2 * i + 2].reshape(256, 1024)
-            b = wg[axis * 4 : axis * 4 + 4].reshape(512, 1024)
-            igb[axis, 2 * i : 2 * i + 2] = dot(a, b, NT).astype(BF16).reshape(2, 128, 512)
-            for kc in range(2):
-                k = 2 * i + kc
-                for t in range(4):
-                    src = igb.at[axis, k, :, pl.ds(t * 128, 128)]
-                    dst = ig.at[:, columns(axis, 0, 0, t)]
-                    if k == 0:
-                        pltpu.make_async_copy(src, dst, local_sem.at[6 + axis]).start()
-                    else:
-                        pltpu.make_async_remote_copy(
-                            src_ref=src, dst_ref=dst, send_sem=o_send.at[axis, k], recv_sem=o_recv.at[axis, k],
-                            device_id=partner(axis, i, kc), device_id_type=MESH,
-                        ).start()
 
     for i in range(4):
         hi, lo = PAIRS[i]
@@ -439,8 +471,7 @@
 
     @pl.when(odd * (1 - foreign) == 1)
     def _():
-        for n in range(2):
-            wait_bytes(rings[n].at[slot], pre_send.at[n])
+        wait_bytes(wg.at[slot, 0], pre_send.at[1])
 
     for copy in sends:
         copy.wait_send()
@@ -464,13 +495,12 @@
         scratch_shapes=[
             V((8, 128, 1024), BF16),
             V((8, 128, 1024), BF16),
-            V((7, 1024, 256), BF16),
             V((2, 8, 128, 512), BF16),
-            V((8, 128, 1024), BF16),
-            V((8, 128, 1024), BF16),
+            V((8, 2, 64, 1024), BF16),
+            V((8, 2, 64, 1024), BF16),
             V((512, 1024), BF16),
             V((1024, 1024), F32),
-            V((1024, 1024), BF16),
+            V((2, 8, 64, 1024), BF16),
             V((2, 8, 128, 512), BF16),
             V((8, 64, 1024), BF16),
             V((8, 64, 1024), BF16),
@@ -507,6 +537,7 @@
             dma((10,)), dma((10,)),
             dma((2, 2, 3)), dma((2, 2, 3)),
             dma((4, 4)), dma((2, 4)),
+            dma((8,)), dma((8,)),
         ],
         compiler_params=pltpu.CompilerParams(
             collective_id=0, has_side_effects=True, vmem_limit_bytes=56 << 20

time: 140 us -> 115 us (0.82)
  Pallas kernels: 133 us -> 108 us
    pallas_call x1, Pallas kernels: 133 us -> 108 us  [local(): pl.pallas_call(kernel, out_shape=(jax.ShapeDtypeStruct((TOKENS, WIDTH), B...]
where the time goes in v2:
time: 115 us; the launch traced here: 114 us
  Pallas kernels  108 us (94%)
  local copies, waits for them, and re-layouts  5.37 us (5%)
    pallas_call x1, Pallas kernels, local(): pl.pallas_call(kernel, out_shape=(jax.ShapeDtypeStruct((TOKENS, WIDTH), B...  108 us
    unnamed x10, local copies, waits for them, and re-layouts  5.37 us

profile of v2, /device:TPU:1, one launch (start us, length us, event | category | flops | bytes accessed | tf_op | source)
XLA Modules:
  0.0 114.3 jit_solution(13873426083272887481)
XLA Ops:
  0.6 108.2 %galore.1 = (bf16[128,8192]{1,0:T(8,128)(2,1)}, bf16[512,1024]{1,0:T(8,128)(2,1)}, f32[4,1024]{1,0:T(4,128)}, f32[4,1024]{1,0:T(4,128)}) custom-call(bf16[128,8192]{1,0:T(8,128)(2,1)} %inp.1, bf16[128,1024]{1,0:T(8,128)(2,1)} %cot.1, bf16[512,1024]{1,0:T(8,128)(2,1)} %w.1, bf16[512,1024]{1,0:T(8,128)(2,1)} %p.1, f32[4,1024]{1,0:T(4,128)} %m_in.1, f32[4,1024]{1,0:T(4,128)} %v_in.1), custom_call_target="tpu_custom_call" | custom-call | tf_op jit(solution)/shard_map/galore/pallas_call | solution.py:485
  108.9 0.0 copy-start
  108.9 0.0 copy-start.2
  108.9 3.2 %copy.14 = bf16[128,8192]{1,0:T(8,128)(2,1)} copy(bf16[128,8192]{1,0:T(8,128)(2,1)} %get-tuple-element.8) | data formatting | bytes 4194304
  112.1 0.0 copy-done
  112.1 0.0 copy-start.1
  112.1 1.0 copy.15
  113.1 0.0 copy-done.2
  113.1 0.6 copy.16
  113.7 0.0 copy-done.1
  113.7 0.6 copy.17
Async XLA Ops:
  108.9 3.2 %copy-start = (bf16[512,1024]{1,0:T(8,128)(2,1)S(1)}, bf16[512,1024]{1,0:T(8,128)(2,1)}, u32[]{:S(2)}) copy-start(bf16[512,1024]{1,0:T(8,128)(2,1)} %get-tuple-element.9) | copy-start | bytes 3145732
  108.9 4.2 %copy-start.2 = (f32[4,1024]{1,0:T(4,128)S(1)}, f32[4,1024]{1,0:T(4,128)}, u32[]{:S(2)}) copy-start(f32[4,1024]{1,0:T(4,128)} %get-tuple-element.10) | copy-start | bytes 49156
  112.1 1.6 %copy-start.1 = (f32[4,1024]{1,0:T(4,128)S(1)}, f32[4,1024]{1,0:T(4,128)}, u32[]{:S(2)}) copy-start(f32[4,1024]{1,0:T(4,128)} %get-tuple-element.11) | copy-start | bytes 49156

commit v3 on v2

--- a/solution.py
+++ b/solution.py
@@ -298,7 +298,6 @@
     wait_bytes(cx.at[1], c_recv.at[0, 0, 1])
     for axis in (1, 0):
         add_inputs(axis, 0, True, False)
-    ring_step(1, 1)
     for i in (1, 3, 2):
         for axis in (1, 0):
             add_inputs(axis, i, False, i == 2)
@@ -324,33 +323,33 @@
                             device_id=partner(axis, i, kc), device_id_type=MESH,
                         ).start()
 
-    basis = pg[...].reshape(1024, 1024)
-
-    for n in range(2):
-        group = slice(n * 4, n * 4 + 4)
-        s0[group] = dot(mb[1 - c, group].reshape(256, 1024), basis).astype(BF16).reshape(4, 64, 1024)
-        send(s0.at[group], r0.at[group], s_send.at[n], s_recv.at[n], partner(0, 0, 1))
+    halves = (pl.ds(0, 512), pl.ds(512, 512))
+
+    def product(core, half):
+        return dot(mb[core].reshape(512, 1024), pg[:, :, :, halves[half]].reshape(1024, 512)).reshape(8, 64, 512)
+
+    for half in range(2):
+        s0[half] = product(1 - c, half).astype(BF16)
+        send(s0.at[half], r0.at[half], s_send.at[half], s_recv.at[half], partner(0, 0, 1))
+    ring_step(1, 1)
+    for half in range(2):
+        a_keep[...] = product(c, half)
+        wait_bytes(r0.at[half], s_recv.at[half])
+        for b in range(8):
+            total = (a_keep[b] + r0[half, b].astype(F32)).astype(BF16)
+            for hh in range(2):
+                if half == 0:
+                    a0[hh, b // 4, b % 4] = total[hh * 32 : hh * 32 + 32]
+                else:
+                    a1[b % 4, b // 4, hh] = total[hh * 32 : hh * 32 + 32]
+        for i in ORDER:
+            hi, lo = PAIRS[i]
+            if half == 0:
+                src, dst = a0.at[flip(h, hi), flip(xl, lo)], ra0
+            else:
+                src, dst = a1.at[flip(yh, hi) * 2 + flip(yl, lo)], ra1
+            send(src, dst.at[i - 1], a_send.at[half, i - 1], a_recv.at[half, i - 1], partner(half, i, 0))
     ring_step(1, 2)
-    for n in range(2):
-        group = slice(n * 4, n * 4 + 4)
-        a_keep[group] = dot(mb[c, group].reshape(256, 1024), basis).reshape(4, 64, 1024)
-    ring_step(1, 3)
-    for n in range(2):
-        wait_bytes(r0.at[n * 4 : n * 4 + 4], s_recv.at[n])
-
-    for b in range(8):
-        xl_, y_ = b // 4, b % 4
-        total = a_keep[b] + r0[b].astype(F32)
-        for hh in range(2):
-            rs = slice(hh * 32, hh * 32 + 32)
-            a0[hh, xl_, y_] = total[rs, 0:512].astype(BF16)
-            a1[y_, xl_, hh] = total[rs, 512:1024].astype(BF16)
-
-    for i in ORDER:
-        hi, lo = PAIRS[i]
-        send(a0.at[flip(h, hi), flip(xl, lo)], ra0.at[i - 1], a_send.at[0, i - 1], a_recv.at[0, i - 1], partner(0, i, 0))
-        send(a1.at[flip(yh, hi) * 2 + flip(yl, lo)], ra1.at[i - 1], a_send.at[1, i - 1], a_recv.at[1, i - 1], partner(1, i, 0))
-    ring_step(1, 4)
     for k in range(1, 8):
         send(mvz.at[z], mvz.at[z], mv_send.at[k - 1], mv_recv.at[k - 1], z_peer(k))
     for n, ref in enumerate((ra0, ra1)):
@@ -362,6 +361,7 @@
         hi, lo = PAIRS[i]
         send(b0.at[flip(yh, hi) * 2 + flip(yl, lo)], rb0.at[i - 1], b_send.at[0, i - 1], b_recv.at[0, i - 1], partner(1, i, 0))
         send(b1.at[flip(xl, lo), flip(h, hi)], rb1.at[i - 1], b_send.at[1, i - 1], b_recv.at[1, i - 1], partner(0, i, 0))
+    ring_step(1, 3)
     for n, ref in enumerate((rb0, rb1)):
         for i in range(3):
             wait_bytes(ref.at[i], b_recv.at[n, i])
@@ -372,8 +372,7 @@
         cs[zz, 4:8, :] = f1[zz * 4 : zz * 4 + 4]
     for k in range(1, 8):
         send(cs.at[(z + k) % 8], rc.at[k - 1], z_send.at[k - 1], z_recv.at[k - 1], z_peer(k))
-    ring_end()
-    return_gradient(0, 3)
+    ring_step(1, 4)
     g = cs[z]
     for k in range(1, 8):
         wait_bytes(rc.at[k - 1], z_recv.at[k - 1])
@@ -381,7 +380,8 @@
     gz[z] = g
     for k in range(1, 8):
         send(gz.at[z], gz.at[z], g_send.at[k - 1], g_recv.at[k - 1], z_peer(k))
-    return_gradient(3, 6)
+    ring_end()
+    return_gradient(0, 4)
     for k in range(1, 8):
         wait_bytes(gz.at[(z - k) % 8], g_recv.at[k - 1])
         wait_bytes(mvz.at[(z - k) % 8], mv_recv.at[k - 1])
@@ -393,7 +393,7 @@
             k = 2 * i + kc
             if k:
                 send(ss.at[0], sr_a.at[k - 1], q_send.at[k - 1], q_recv.at[k - 1], partner(0, i, kc))
-    return_gradient(6, 8)
+    return_gradient(4, 8)
     total = ss[0]
     for k in range(1, 8):
         wait_bytes(sr_a.at[k - 1], q_recv.at[k - 1])
@@ -419,8 +419,6 @@
         df[zz * 4 : zz * 4 + 4, 512:1024] = direction[4:8]
     dall[xl, y, c, h] = df[...].astype(BF16)
 
-    halves = (pl.ds(0, 512), pl.ds(512, 512))
-    own = dall.at[xl, y, c, h]
     for i in ORDER:
         for axis in range(2):
             piece = dall.at[xl, y, c, h, :, halves[axis]]
@@ -502,9 +500,9 @@
             V((1024, 1024), F32),
             V((2, 8, 64, 1024), BF16),
             V((2, 8, 128, 512), BF16),
-            V((8, 64, 1024), BF16),
-            V((8, 64, 1024), BF16),
-            V((8, 64, 1024), F32),
+            V((2, 8, 64, 512), BF16),
+            V((2, 8, 64, 512), BF16),
+            V((8, 64, 512), F32),
             V((2, 2, 4, 32, 512), BF16),
             V((4, 2, 2, 32, 512), BF16),
             V((3, 4, 32, 512), BF16),

time: 115 us -> 114 us (level)
  no operation moved by 1% of the time
where the time goes in v3:
time: 114 us; the launch traced here: 113 us
  Pallas kernels  107 us (94%)
  local copies, waits for them, and re-layouts  5.37 us (5%)
    pallas_call x1, Pallas kernels, local(): pl.pallas_call(kernel, out_shape=(jax.ShapeDtypeStruct((TOKENS, WIDTH), B...  107 us
    unnamed x10, local copies, waits for them, and re-layouts  5.37 us

profile of v3, /device:TPU:1, one launch (start us, length us, event | category | flops | bytes accessed | tf_op | source)
XLA Modules:
  0.0 113.4 jit_solution(6930837066989301658)
XLA Ops:
  0.6 107.4 %galore.1 = (bf16[128,8192]{1,0:T(8,128)(2,1)}, bf16[512,1024]{1,0:T(8,128)(2,1)}, f32[4,1024]{1,0:T(4,128)}, f32[4,1024]{1,0:T(4,128)}) custom-call(bf16[128,8192]{1,0:T(8,128)(2,1)} %inp.1, bf16[128,1024]{1,0:T(8,128)(2,1)} %cot.1, bf16[512,1024]{1,0:T(8,128)(2,1)} %w.1, bf16[512,1024]{1,0:T(8,128)(2,1)} %p.1, f32[4,1024]{1,0:T(4,128)} %m_in.1, f32[4,1024]{1,0:T(4,128)} %v_in.1), custom_call_target="tpu_custom_call" | custom-call | tf_op jit(solution)/shard_map/galore/pallas_call | solution.py:483
  108.0 0.0 copy-start
  108.0 0.0 copy-start.2
  108.0 3.2 %copy.14 = bf16[128,8192]{1,0:T(8,128)(2,1)} copy(bf16[128,8192]{1,0:T(8,128)(2,1)} %get-tuple-element.8) | data formatting | bytes 4194304
  111.2 0.0 copy-done
  111.2 0.0 copy-start.1
  111.2 1.0 copy.15
  112.2 0.0 copy-done.2
  112.2 0.6 copy.16
  112.8 0.0 copy-done.1
  112.8 0.6 copy.17
Async XLA Ops:
  108.0 3.2 %copy-start = (bf16[512,1024]{1,0:T(8,128)(2,1)S(1)}, bf16[512,1024]{1,0:T(8,128)(2,1)}, u32[]{:S(2)}) copy-start(bf16[512,1024]{1,0:T(8,128)(2,1)} %get-tuple-element.9) | copy-start | bytes 3145732
  108.0 4.2 %copy-start.2 = (f32[4,1024]{1,0:T(4,128)S(1)}, f32[4,1024]{1,0:T(4,128)}, u32[]{:S(2)}) copy-start(f32[4,1024]{1,0:T(4,128)} %get-tuple-element.10) | copy-start | bytes 49156
  111.2 1.6 %copy-start.1 = (f32[4,1024]{1,0:T(4,128)S(1)}, f32[4,1024]{1,0:T(4,128)}, u32[]{:S(2)}) copy-start(f32[4,1024]{1,0:T(4,128)} %get-tuple-element.11) | copy-start | bytes 49156

commit v4 on v3

--- a/solution.py
+++ b/solution.py
@@ -90,7 +90,7 @@
     barrier = pltpu.get_barrier_semaphore()
     peers = [partner(0, i, kc) for i in range(4) for kc in range(2) if (i, kc) != (0, 0)]
     peers += [partner(1, i, kc) for i in range(1, 4) for kc in range(2)]
-    peers += [z_peer(k) for k in range(1, 8)]
+    peers += [z_peer(k) for k in (1, 7)]
     for peer in peers:
         pl.semaphore_signal(barrier, inc=1, device_id=peer, device_id_type=MESH)
 

time: 114 us -> 114 us (level)
  no operation moved by 1% of the time
where the time goes in v4:
time: 114 us; the launch traced here: 113 us
  Pallas kernels  107 us (94%)
  local copies, waits for them, and re-layouts  5.37 us (5%)
    pallas_call x1, Pallas kernels, local(): pl.pallas_call(kernel, out_shape=(jax.ShapeDtypeStruct((TOKENS, WIDTH), B...  107 us
    unnamed x10, local copies, waits for them, and re-layouts  5.37 us

profile of v4, /device:TPU:1, one launch (start us, length us, event | category | flops | bytes accessed | tf_op | source)
XLA Modules:
  0.0 113.4 jit_solution(11060679558261417606)
XLA Ops:
  0.6 107.3 %galore.1 = (bf16[128,8192]{1,0:T(8,128)(2,1)}, bf16[512,1024]{1,0:T(8,128)(2,1)}, f32[4,1024]{1,0:T(4,128)}, f32[4,1024]{1,0:T(4,128)}) custom-call(bf16[128,8192]{1,0:T(8,128)(2,1)} %inp.1, bf16[128,1024]{1,0:T(8,128)(2,1)} %cot.1, bf16[512,1024]{1,0:T(8,128)(2,1)} %w.1, bf16[512,1024]{1,0:T(8,128)(2,1)} %p.1, f32[4,1024]{1,0:T(4,128)} %m_in.1, f32[4,1024]{1,0:T(4,128)} %v_in.1), custom_call_target="tpu_custom_call" | custom-call | tf_op jit(solution)/shard_map/galore/pallas_call | solution.py:483
  108.0 0.0 copy-start
  108.0 0.0 copy-start.2
  108.0 3.2 %copy.14 = bf16[128,8192]{1,0:T(8,128)(2,1)} copy(bf16[128,8192]{1,0:T(8,128)(2,1)} %get-tuple-element.8) | data formatting | bytes 4194304
  111.2 0.0 copy-done
  111.2 0.0 copy-start.1
  111.2 1.0 copy.15
  112.1 0.0 copy-done.2
  112.1 0.6 copy.16
  112.7 0.0 copy-done.1
  112.7 0.6 copy.17
Async XLA Ops:
  108.0 3.2 %copy-start = (bf16[512,1024]{1,0:T(8,128)(2,1)S(1)}, bf16[512,1024]{1,0:T(8,128)(2,1)}, u32[]{:S(2)}) copy-start(bf16[512,1024]{1,0:T(8,128)(2,1)} %get-tuple-element.9) | copy-start | bytes 3145732
  108.0 4.2 %copy-start.2 = (f32[4,1024]{1,0:T(4,128)S(1)}, f32[4,1024]{1,0:T(4,128)}, u32[]{:S(2)}) copy-start(f32[4,1024]{1,0:T(4,128)} %get-tuple-element.10) | copy-start | bytes 49156
  111.2 1.6 %copy-start.1 = (f32[4,1024]{1,0:T(4,128)S(1)}, f32[4,1024]{1,0:T(4,128)}, u32[]{:S(2)}) copy-start(f32[4,1024]{1,0:T(4,128)} %get-tuple-element.11) | copy-start | bytes 49156
